TPU v7x, 32 devices: a whole 2x2x4 slice. The times are simulated.
32 devices in a mesh: groups: 2 (over x), band: 16 (over z, y, core).
Axes of the slice: x: 2, y: 2, z: 4, core: 2. Of those that a mesh axis runs over, the one named last changes fastest.
Arguments:
- records: bfloat16 [8192, 4096], P(None, ('groups', 'band')), parts along dimension 1, may hold values from -40 to 40
- source: int32 [4096], P(('groups', 'band')), parts along dimension 0, may hold values from 0 to 133, as said below
- weight: float32 [4096], P(('groups', 'band')), parts along dimension 0, may hold values from 0 to 1
- gap_mask: int32 [4096], P(('groups', 'band')), parts along dimension 0, may hold values from 0 to 1, as said below
Outputs:
- cleaned: bfloat16 [8, 1024, 4096], P(None, 'band', 'groups'), parts along dimension 2
- tiles: bfloat16 [32, 2, 2, 1024, 1024], P(('groups', 'band')), parts along dimension 0
There are 2 independent parts, one for each index of `groups`. A program takes and returns all parts, laid end to end along the dimension named above; each array names one. Nothing has to cross between parts.
Inputs may be any that keep to these rules, and one draw needn't show every extreme that they name: `source`: for sample i of a device's 128 samples the value lies in i .. i + 6; it is i at a device's first sample and i + 6 at its last. `gap_mask`: on each device's 128 samples the zeros form one run of at most 32 samples that never covers the device's first sample; some device has a run of exactly that length.
All inputs are finite; a program needn't handle non-finite values.
Results may differ from a plain program's by a relative error of at most 0.0052.
Values may be sent and summed in bfloat16 or wider, within the bound.
A program may use at most 64 MiB of HBM per device.

v0:
```python
import math

import jax
import jax.numpy as jnp
from jax import lax
from jax.sharding import PartitionSpec as P

BLOCKS = 8
HALO = 8
FB = 64
F_LO = 16


epsilon = 1e-06


def passed_along(block, axis, distance):
    devices = range(lax.axis_size(axis))
    route = [(i - distance, i) for i in devices if i - distance in devices]
    return lax.ppermute(block, axis, route)


def harmonic_matrix(acquisition_moments, spectral_line_total, trace_duration):
    cycles_per_second = F_LO + jnp.arange(spectral_line_total, dtype=jnp.int32)
    angle_step = acquisition_moments[:, None] * cycles_per_second[None, :] % trace_duration
    phase_angle = angle_step.astype(jnp.float32) * (2.0 * math.pi / trace_duration)
    return jnp.concatenate([jnp.cos(phase_angle), -jnp.sin(phase_angle)], axis=1).astype(
        jnp.bfloat16
    )


def spread_matrix(source, weight, gap_mask, span):
    positions = jnp.arange(span, dtype=jnp.int32)[:, None]
    lower_hit = (positions == source[..., None, :]).astype(jnp.float32)
    upper_hit = (positions == source[..., None, :] + 1).astype(jnp.float32)
    mask_float = gap_mask.astype(jnp.float32)[..., None, :]
    return mask_float * (
        (1.0 - weight[..., None, :]) * lower_hit + weight[..., None, :] * upper_hit
    )


def whiten(spectra):
    values = spectra.astype(jnp.float32)
    band_power = jnp.sum(values * values, axis=(-3, -2)) / values.shape[-2]
    return (values * lax.rsqrt(band_power + epsilon)[..., None, None, :]).astype(jnp.bfloat16)


def pair_tiles(own_block, following):
    stacked_bins = own_block.shape[0] * own_block.shape[1]
    left_side = own_block.reshape(stacked_bins, -1).astype(jnp.float32)

    def columns(spectra):
        return jnp.stack(
            [spectra.reshape(stacked_bins, -1), jnp.concatenate([spectra[1], -spectra[0]], axis=0)]
        )

    right_side = jnp.concatenate([columns(own_block), columns(following)], axis=0).astype(
        jnp.float32
    )
    pair_tile = jnp.einsum("fi,pfj->pij", left_side, right_side, precision=lax.Precision.HIGHEST)
    width_out = left_side.shape[1]
    return (pair_tile / own_block.shape[1]).astype(jnp.bfloat16).reshape(2, 2, width_out, width_out)


def per_device(records, source, weight, gap_mask):
    devices = lax.axis_size("band")
    channels, shard_len = records.shape
    block_width = channels // BLOCKS
    mask_float = gap_mask.astype(jnp.float32)
    carried = passed_along(records[:, :HALO], "band", -1)
    padded = jnp.concatenate([records, carried], axis=1).astype(jnp.float32)
    spreader = spread_matrix(source, weight, gap_mask, shard_len + HALO)
    resampled = jnp.dot(padded, spreader, precision=lax.Precision.HIGHEST)
    totals, valid_count = lax.psum((jnp.sum(resampled, axis=1), jnp.sum(mask_float)), "band")
    local_clean = (mask_float * (resampled - (totals / valid_count)[:, None])).astype(jnp.bfloat16)
    cleaned = lax.all_to_all(
        local_clean.reshape(BLOCKS, block_width, shard_len),
        "band",
        split_axis=1,
        concat_axis=2,
        tiled=True,
    )
    taper_span = cleaned.shape[2]
    stripe_rows = cleaned.reshape(-1, taper_span)
    band_count = devices // BLOCKS
    spectral_line_total = FB * band_count
    segment_span = min(1024, taper_span)

    def accumulate(block_step, running):
        first_moment = block_step * segment_span
        window_rows = lax.dynamic_slice_in_dim(stripe_rows, first_moment, segment_span, 1).astype(
            jnp.float32
        )
        acquisition_moments = first_moment + jnp.arange(segment_span, dtype=jnp.int32)
        kernel_part = harmonic_matrix(acquisition_moments, spectral_line_total, taper_span).astype(
            jnp.float32
        )
        return running + jnp.dot(window_rows, kernel_part, precision=lax.Precision.HIGHEST)

    spectrum = lax.fori_loop(
        0,
        taper_span // segment_span,
        accumulate,
        jnp.zeros((stripe_rows.shape[0], 2 * spectral_line_total), jnp.float32),
    )
    spectrum = spectrum.astype(jnp.bfloat16)
    band_parts = spectrum.reshape(BLOCKS, -1, 2, band_count, FB).transpose(3, 0, 2, 4, 1)
    stripe_width = band_parts.shape[4]
    arrived = lax.all_to_all(
        band_parts.reshape(devices, 2, FB, stripe_width),
        "band",
        split_axis=0,
        concat_axis=3,
        tiled=True,
    )
    own_block = whiten(arrived[0])
    neighbour = passed_along(own_block, "band", -1)
    position = lax.axis_index("band") % BLOCKS
    following = jnp.where(position == BLOCKS - 1, jnp.zeros_like(neighbour), neighbour)
    return (cleaned, pair_tiles(own_block, following)[None])


def solution(mesh):
    placed = (
        P(None, ("groups", "band")),
        P(("groups", "band")),
        P(("groups", "band")),
        P(("groups", "band")),
    )
    return jax.shard_map(
        per_device,
        mesh=mesh,
        in_specs=placed,
        out_specs=(P(None, "band", "groups"), P(("groups", "band"), None, None, None, None)),
        check_vma=False,
    )
```

profile of v0, /device:TPU:1, one launch (start us, length us, event | category | flops | bytes accessed | tf_op | source)
XLA Modules:
  0.0 200.6 jit_solution(10814552097959065287)
XLA Ops:
  0.6 0.0 copy-start
  0.6 0.0 copy-start.5
  0.7 0.0 copy-start.4
  0.7 2.0 copy.41
  2.6 2.0 collective-permute-start
  4.6 0.7 broadcast_add_fusion
  5.3 0.7 broadcast_subtract_fusion
  5.9 0.7 convert_element_type.99
  6.6 1.3 convert_reduce_fusion
  7.9 2.0 collective-permute-done
  9.8 1.7 copy.30
  11.5 0.0 copy-done
  11.5 0.0 copy-done.5
  11.5 0.0 copy-done.4
  11.5 7.0 %fusion.39 = (f32[8192]{0:T(1024)S(1)}, f32[8192,128]{1,0:T(8,128)}) fusion(f32[128]{0:T(128)S(1)} %copy-done.4, s32[128]{0:T(128)S(1)} %broadcast_add_fusion, f32[128]{0:T(128)S(1)} %broadcast_subtract_fusion, s32[128]{0:T(128)S(1)} %copy-done.5, f32[128]{0:T(128)S(1)} %convert_element_type.99, bf16[8192,8]{1,0:T(8,128)(2,1)} %copy.30, ...), kind=kOutput, calls=%fused_computation.70 | convolution fusion | flops 1716877312 | bytes 6457856 | tf_op jit(solution)/shard_map/dot_general | solution.py:73
  18.6 57.7 %all-reduce = (f32[8192]{0:T(1024)S(1)}, f32[]{:T(128)}) all-reduce(f32[8192]{0:T(1024)S(1)} %get-tuple-element.126, f32[]{:T(128)} %convert_reduce_fusion), channel_id=1, replica_groups=mesh['groups'=2,'band'=16] {'band'}, use_global_device_ids=true, to_apply=%region_1.0 | all-reduce | flops 8193 | bytes 65544 | tf_op jit(solution)/shard_map/psum | solution.py:74
  76.3 0.7 broadcast_divide_fusion
  77.0 2.9 %multiply_convert_fusion.1 = bf16[8192,128]{1,0:T(8,128)(2,1)S(1)} fusion(f32[8192,128]{1,0:T(8,128)} %get-tuple-element.127, f32[8192]{0:T(1024)S(1)} %broadcast_divide_fusion, f32[128]{0:T(128)S(1)} %convert_element_type.99), kind=kLoop, calls=%fused_computation.24 | loop fusion | flops 3145728 | bytes 6324736 | tf_op jit(solution)/shard_map/convert_element_type | solution.py:75
  79.8 2.7 %copy.31 = bf16[8,1024,128]{2,0,1:T(8,128)(2,1)} copy(bf16[8,1024,128]{2,1,0:T(8,128)(2,1)S(1)} %bitcast.49) | data formatting | bytes 4194304 | tf_op jit(solution)/shard_map/reshape | solution.py:77
  82.5 8.5 %all-to-all-start = ((bf16[8,1024,128]{2,0,1:T(8,128)(2,1)}), bf16[8,1024,128]{2,0,1:T(8,128)(2,1)S(1)}, u32[]{:S(2)}, u32[]{:S(2)}) async-start(bf16[8,1024,128]{2,0,1:T(8,128)(2,1)} %copy.31), calls=%async_computation | async-start | bytes 4194304 | tf_op jit(solution)/shard_map/all_to_all | solution.py:76
  91.0 41.5 %all-to-all-done = bf16[8,1024,128]{2,0,1:T(8,128)(2,1)S(1)} async-done(((bf16[8,1024,128]{2,0,1:T(8,128)(2,1)}), bf16[8,1024,128]{2,0,1:T(8,128)(2,1)S(1)}, u32[]{:S(2)}, u32[]{:S(2)}) %all-to-all-start) | async-done | bytes 2097184 | tf_op jit(solution)/shard_map/all_to_all | solution.py:76
  132.5 0.0 copy-start.1
  132.6 1.3 copy-done.1
  133.9 2.9 %copy.32 = bf16[8,64,16,128]{3,2,1,0:T(8,128)(2,1)S(1)} copy(bf16[8,64,16,128]{3,0,1,2:T(8,128)(2,1)} %bitcast.51) | data formatting | bytes 4194304 | tf_op jit(solution)/shard_map/all_to_all | solution.py:76
  136.8 1.9 copy.44
  138.7 8.7 %while.16 = (s32[]{:T(128)}, f32[512,256]{1,0:T(8,128)S(1)}, bf16[512,2048]{1,0:T(8,128)(2,1)}, s32[]{:T(128)}, s32[]{:T(128)}, /*index=5*/s32[]{:T(128)}, s32[]{:T(128)}) while((s32[]{:T(128)}, f32[512,256]{1,0:T(8,128)S(1)}, bf16[512,2048]{1,0:T(8,128)(2,1)}, s32[]{:T(128)}, s32[]{:T(128)}, /*index=5*/s32[]{:T(128)}, ...), condition=%wide.region_5.6_spmd.clone, body=%wide.region_4.5_spmd.clone.sunk | while | flops 271975552 | bytes 3155093 | solution.py:100
  138.7 2.5 %cosine_convert_fusion.2 = (bf16[1024,128]{1,0:T(8,128)(2,1)S(1)}, bf16[1024,128]{1,0:T(8,128)(2,1)S(1)}) fusion(s32[128]{0:T(128)S(1)} %iota_add_fusion.4, s32[1024]{0:T(1024)S(1)} %iota_add_fusion.5), kind=kLoop, calls=%fused_computation.14.clone.1 | loop fusion | flops 2228224 | bytes 528896 | tf_op jit(solution)/shard_map/convert
  141.2 1.8 convolution_add_fusion.2
  143.0 2.5 %cosine_convert_fusion.2 = (bf16[1024,128]{1,0:T(8,128)(2,1)S(1)}, bf16[1024,128]{1,0:T(8,128)(2,1)S(1)}) fusion(s32[128]{0:T(128)S(1)} %iota_add_fusion.4, s32[1024]{0:T(1024)S(1)} %iota_add_fusion.5), kind=kLoop, calls=%fused_computation.14.clone.1 | loop fusion | flops 2228224 | bytes 528896 | tf_op jit(solution)/shard_map/convert
  145.5 1.8 convolution_add_fusion.2
  147.4 0.2 reshape.99
  147.6 0.1 copy.34
  147.8 1.1 reshape.108
  148.9 10.8 %all-to-all-start.1 = ((bf16[16,2,4096]{2,1,0:T(2,128)(2,1)}), bf16[16,2,4096]{2,1,0:T(2,128)(2,1)S(1)}, u32[]{:S(2)}, u32[]{:S(2)}) async-start(bf16[16,2,4096]{2,1,0:T(2,128)(2,1)} %reshape.108), calls=%async_computation.1 | async-start | bytes 524288 | tf_op jit(solution)/shard_map/all_to_all | solution.py:109
  159.7 2.3 %all_to_all.23 = bf16[8,64,2048]{2,1,0:T(8,128)(2,1)} reshape(bf16[8,64,16,128]{3,2,1,0:T(8,128)(2,1)S(1)} %copy.32) | data formatting | bytes 4194304 | tf_op jit(solution)/shard_map/all_to_all | solution.py:76
  162.0 7.2 %all-to-all-done.1 = bf16[16,2,4096]{2,1,0:T(2,128)(2,1)S(1)} async-done(((bf16[16,2,4096]{2,1,0:T(2,128)(2,1)}), bf16[16,2,4096]{2,1,0:T(2,128)(2,1)S(1)}, u32[]{:S(2)}, u32[]{:S(2)}) %all-to-all-start.1) | async-done | bytes 262176 | tf_op jit(solution)/shard_map/all_to_all | solution.py:109
  169.2 0.3 reshape.109
  169.6 0.2 fusion.13
  169.8 0.1 convert_bitcast_fusion
  169.9 0.1 rsqrt.11
  170.0 0.1 copy.36
  170.1 1.0 multiply_convert_fusion.2
  171.1 2.6 %collective-permute-start.1 = (bf16[2,64,1024]{1,2,0:T(8,128)(2,1)}, bf16[2,64,1024]{1,2,0:T(8,128)(2,1)}, u32[]{:S(2)}, u32[]{:S(2)}) collective-permute-start(bf16[2,64,1024]{1,2,0:T(8,128)(2,1)} %multiply_convert_fusion.2), channel_id=1, source_target_pairs={{1,0},{2,1},{3,2},{4,3},{5,4},{6,5},{7,6},{8,7},{9,8},{10,9},{11,1... | collective-permute-start | bytes 786440 | tf_op jit(solution)/shard_map/ppermute | solution.py:20
  173.6 1.8 slice_bitcast_fusion.1
  175.4 0.5 copy.39
  175.9 0.8 copy.35
  176.7 0.0 copy-start.2
  176.8 1.1 reshape.103
  177.9 0.0 copy-start.3
  177.9 0.6 reshape.101
  178.4 0.2 multiply_convert_fusion.4
  178.6 3.2 %collective-permute-done.1 = bf16[2,64,1024]{1,2,0:T(8,128)(2,1)} collective-permute-done((bf16[2,64,1024]{1,2,0:T(8,128)(2,1)}, bf16[2,64,1024]{1,2,0:T(8,128)(2,1)}, u32[]{:S(2)}, u32[]{:S(2)}) %collective-permute-start.1) | collective-permute-done | bytes 262176 | tf_op jit(solution)/shard_map/ppermute | solution.py:20
  181.9 1.1 broadcast_select_fusion
  183.0 0.2 copy.37
  183.2 0.1 slice_bitcast_fusion
  183.2 0.2 copy.38
  183.4 0.0 copy-done.2
  183.4 0.3 maximum_bitcast_fusion
  183.7 0.0 copy-done.3
  183.7 5.6 %multiply_convert_fusion = bf16[4,1024,1024]{2,1,0:T(8,128)(2,1)} fusion(bf16[1,128,1024]{1,2,0:T(8,128)(2,1)S(1)} %get-tuple-element.129, bf16[1,128,1024]{1,2,0:T(8,128)(2,1)S(1)} %copy.38, bf16[1,128,1024]{1,2,0:T(8,128)(2,1)S(1)} %get-tuple-element.128, bf16[1,128,1024]{1,2,0:T(8,128)(2,1)S(1)} %multiply_convert_fusion.4, ...), kind=kOutput, calls=%fused_computation.19 | convolution fusion | flops 1083965440 | bytes 9965568 | tf_op jit(solution)/shard_map/fi,pfj->pij/dot_general | solution.py:60
  189.3 11.3 %copy.40 = bf16[1,2,2,1024,1024]{4,3,2,1,0:T(8,128)(2,1)} copy(bf16[1,2,2,1024,1024]{3,4,2,1,0:T(8,128)(2,1)} %bitcast.50) | data formatting | bytes 16777216
  (7 shorter events, 0.0 us)
Async XLA Ops:
  0.6 10.9 %copy-start = (bf16[8192,128]{1,0:T(8,128)(2,1)S(1)}, bf16[8192,128]{1,0:T(8,128)(2,1)}, u32[]{:S(2)}) copy-start(bf16[8192,128]{1,0:T(8,128)(2,1)} %param.6) | copy-start | bytes 6291460
  0.6 10.9 %copy-start.5 = (s32[128]{0:T(128)S(1)}, s32[128]{0:T(128)}, u32[]{:S(2)}) copy-start(s32[128]{0:T(128)} %param.7) | copy-start | bytes 1540
  0.7 10.9 %copy-start.4 = (f32[128]{0:T(128)S(1)}, f32[128]{0:T(128)}, u32[]{:S(2)}) copy-start(f32[128]{0:T(128)} %param.8) | copy-start | bytes 1540
  2.6 7.2 %collective-permute-start = (bf16[8192,8]{0,1:T(8,128)(2,1)S(1)}, bf16[8192,8]{0,1:T(8,128)(2,1)S(1)}, u32[]{:S(2)}, u32[]{:S(2)}) collective-permute-start(bf16[8192,8]{0,1:T(8,128)(2,1)S(1)} %copy.41), channel_id=1, source_target_pairs={{1,0},{2,1},{3,2},{4,3},{5,4},{6,5},{7,6},{8,7},{9,8},{10,9},{11,1... | collective-permute-start | bytes 393224 | tf_op jit(solution)/shard_map/ppermute | solution.py:20
  82.5 50.1 %all-to-all-start = ((bf16[8,1024,128]{2,0,1:T(8,128)(2,1)}), bf16[8,1024,128]{2,0,1:T(8,128)(2,1)S(1)}, u32[]{:S(2)}, u32[]{:S(2)}) async-start(bf16[8,1024,128]{2,0,1:T(8,128)(2,1)} %copy.31), calls=%async_computation | async-start | bytes 4194304 | tf_op jit(solution)/shard_map/all_to_all | solution.py:76
  132.5 1.3 copy-start.1
  148.9 20.3 %all-to-all-start.1 = ((bf16[16,2,4096]{2,1,0:T(2,128)(2,1)}), bf16[16,2,4096]{2,1,0:T(2,128)(2,1)S(1)}, u32[]{:S(2)}, u32[]{:S(2)}) async-start(bf16[16,2,4096]{2,1,0:T(2,128)(2,1)} %reshape.108), calls=%async_computation.1 | async-start | bytes 524288 | tf_op jit(solution)/shard_map/all_to_all | solution.py:109
  171.1 10.8 %collective-permute-start.1 = (bf16[2,64,1024]{1,2,0:T(8,128)(2,1)}, bf16[2,64,1024]{1,2,0:T(8,128)(2,1)}, u32[]{:S(2)}, u32[]{:S(2)}) collective-permute-start(bf16[2,64,1024]{1,2,0:T(8,128)(2,1)} %multiply_convert_fusion.2), channel_id=1, source_target_pairs={{1,0},{2,1},{3,2},{4,3},{5,4},{6,5},{7,6},{8,7},{9,8},{10,9},{11,1... | collective-permute-start | bytes 786440 | tf_op jit(solution)/shard_map/ppermute | solution.py:20
  176.7 6.7 %copy-start.2 = (bf16[64,1024]{0,1:T(8,128)(2,1)S(1)}, bf16[64,1024]{0,1:T(8,128)(2,1)}, u32[]{:S(2)}) copy-start(bf16[64,1024]{0,1:T(8,128)(2,1)} %get-tuple-element.123) | copy-start | bytes 393220
  177.9 5.8 %copy-start.3 = (f32[128,1024]{1,0:T(8,128)S(1)}, f32[128,1024]{1,0:T(8,128)}, u32[]{:S(2)}) copy-start(f32[128,1024]{1,0:T(8,128)} %reshape.103) | copy-start | bytes 1572868
where the time goes:
time: 201 us
  blocking collectives  57.7 us (29%)
  waiting for transfers between devices  53.9 us (27%)
  local copies, waits for them, and re-layouts  31.4 us (16%)
  starting transfers between devices  23.9 us (12%)
  other arithmetic  16.5 us (8%)
  matrix products  16.2 us (8%)
    psum x1, blocking collectives, per_device(): lax.psum((jnp.sum(resampled, axis=1), jnp.sum(mask_float)), 'band')  57.7 us
    all_to_all x1, waiting for transfers between devices, per_device(): lax.all_to_all(local_clean.reshape(BLOCKS, block_width, shard_len), 'band...  41.5 us
    unnamed x17, local copies, waits for them, and re-layouts  18 us
    all_to_all x1, starting transfers between devices, per_device(): lax.all_to_all(band_parts.reshape(devices, 2, FB, stripe_width), 'band',...  10.8 us
    all_to_all x1, starting transfers between devices, per_device(): lax.all_to_all(local_clean.reshape(BLOCKS, block_width, shard_len), 'band...  8.54 us
    all_to_all x1, waiting for transfers between devices, per_device(): lax.all_to_all(band_parts.reshape(devices, 2, FB, stripe_width), 'band',...  7.21 us
    dot_general x1, matrix products, per_device(): resampled = jnp.dot(padded, spreader, precision=lax.Precision.HIGHEST)  7.04 us
    dot_general x1, matrix products, pair_tiles(): jnp.einsum('fi,pfj->pij', left_side, right_side, precision=lax.Precision....  5.58 us
  transfers between devices with their start and end apart: 4, of which 4 were waited for; matrix products, arithmetic and copies ran while one was open for 4% of the time, Pallas kernels for 0%

commit v1 on v0

--- a/solution.py
+++ b/solution.py
@@ -1,8 +1,11 @@
+import functools
 import math
 
 import jax
 import jax.numpy as jnp
 from jax import lax
+from jax.experimental import pallas as pl
+from jax.experimental.pallas import tpu as pltpu
 from jax.sharding import PartitionSpec as P
 
 BLOCKS = 8
@@ -62,7 +65,7 @@
     return (pair_tile / own_block.shape[1]).astype(jnp.bfloat16).reshape(2, 2, width_out, width_out)
 
 
-def per_device(records, source, weight, gap_mask):
+def per_device_collectives(records, source, weight, gap_mask):
     devices = lax.axis_size("band")
     channels, shard_len = records.shape
     block_width = channels // BLOCKS
@@ -120,6 +123,369 @@
     return (cleaned, pair_tiles(own_block, following)[None])
 
 
+LOOKAHEAD = 3
+MESH = pl.DeviceIdType.MESH
+
+
+def half_turn_cosine(steps, turn):
+    folded = jnp.minimum(steps, turn - steps).astype(jnp.float32)
+    y = (0.25 * turn - folded) * (2.0 * math.pi / turn)
+    y2 = y * y
+    total = jnp.full_like(y, -1.0 / 39916800.0)
+    for term in (1.0 / 362880.0, -1.0 / 5040.0, 1.0 / 120.0, -1.0 / 6.0, 1.0):
+        total = total * y2 + term
+    return total * y
+
+
+def exchange_kernel(
+    n,
+    records,
+    source,
+    weight,
+    gap_mask,
+    cleaned,
+    own_out,
+    next_out,
+    info,
+    infos,
+    raw,
+    resampled,
+    clean,
+    table,
+    spectra,
+    own,
+    following,
+    info_send,
+    info_recv,
+    raw_send,
+    raw_recv,
+    raw_local,
+    clean_sem,
+    spec_send,
+    spec_recv,
+    pass_send,
+    pass_recv,
+):
+    me = lax.axis_index("band")
+    shard_len = records.shape[1]
+    block_width = records.shape[0] // BLOCKS
+    stripe = block_width // n
+    bands = n // BLOCKS
+    span = n * shard_len
+    my_block = lax.rem(me, BLOCKS)
+
+    barrier = pltpu.get_barrier_semaphore()
+
+    def greet(j, carry):
+        pl.semaphore_signal(
+            barrier, inc=1, device_id={"band": lax.rem(me + j, n)}, device_id_type=MESH
+        )
+        return carry
+
+    lax.fori_loop(1, n, greet, 0)
+
+    row = lax.broadcasted_iota(jnp.int32, (HALO, shard_len), 0)
+    lane = lax.broadcasted_iota(jnp.int32, (HALO, shard_len), 1)
+    offset = source[...] - lane
+    mask_row = gap_mask[...].astype(jnp.float32)
+    upper = weight[...]
+    info[:HALO] = mask_row * (
+        jnp.where(offset == row, 1.0 - upper, 0.0) + jnp.where(offset + 1 == row, upper, 0.0)
+    )
+    info[HALO:] = jnp.broadcast_to(mask_row, (HALO, shard_len))
+    infos[me] = info[...]
+
+    def local_copy(k):
+        start = pl.multiple_of(k * block_width + me * stripe, stripe)
+        return pltpu.make_async_copy(
+            records.at[pl.ds(start, stripe)], raw.at[k, me], raw_local.at[k]
+        )
+
+    def start_local(k, carry):
+        local_copy(k).start()
+        return carry
+
+    lax.fori_loop(0, BLOCKS, start_local, 0)
+    pl.semaphore_wait(barrier, n - 1)
+
+    def send_info(j, carry):
+        pltpu.make_async_remote_copy(
+            src_ref=info,
+            dst_ref=infos.at[me],
+            send_sem=info_send,
+            recv_sem=info_recv,
+            device_id={"band": lax.rem(me + j, n)},
+            device_id_type=MESH,
+        ).start()
+        return carry
+
+    lax.fori_loop(1, n, send_info, 0)
+
+    def send_block(k):
+        def send(j, carry):
+            to = lax.rem(me + j, n)
+            start = pl.multiple_of(k * block_width + to * stripe, stripe)
+            pltpu.make_async_remote_copy(
+                src_ref=records.at[pl.ds(start, stripe)],
+                dst_ref=raw.at[k, me],
+                send_sem=raw_send,
+                recv_sem=raw_recv.at[k],
+                device_id={"band": to},
+                device_id_type=MESH,
+            ).start()
+            return carry
+
+        lax.fori_loop(1, n, send, 0)
+
+    for k in range(BLOCKS - 1, BLOCKS - 1 - LOOKAHEAD, -1):
+        send_block(k)
+
+    for k in range(BLOCKS):
+        raw[k, n] = jnp.zeros((stripe, shard_len), raw.dtype)
+
+    moments = 128
+
+    def fill(step, carry):
+        shape = (moments, 2 * FB)
+        t = step * moments + lax.broadcasted_iota(jnp.int32, shape, 0)
+        column = lax.broadcasted_iota(jnp.int32, shape, 1)
+        part = column // FB
+        for q in range(bands):
+            f = F_LO + q * FB + column - part * FB
+            steps = (t * f + part * (span // 4)) & (span - 1)
+            start = pl.multiple_of(step * moments, moments)
+            table[pl.ds(start, moments), q * 2 * FB : (q + 1) * 2 * FB] = half_turn_cosine(
+                steps, span
+            ).astype(table.dtype)
+        return carry
+
+    lax.fori_loop(0, span // moments, fill, 0)
+
+    others = pl.ds(0, n - 1)
+    pltpu.make_async_copy(infos.at[others], infos.at[others], info_recv).wait()
+    count = jnp.sum(infos[:, HALO, :])
+
+    lane = lax.broadcasted_iota(jnp.int32, (stripe, shard_len), 1)
+
+    def one_block(i, carry):
+        k = BLOCKS - 1 - i
+
+        @pl.when(k >= LOOKAHEAD)
+        def _():
+            send_block(k - LOOKAHEAD)
+
+        pltpu.make_async_copy(raw.at[k, others], raw.at[k, others], raw_recv.at[k]).wait()
+        local_copy(k).wait()
+
+        def resample(s, total):
+            here = raw[k, s].astype(jnp.float32)
+            after = raw[k, s + 1].astype(jnp.float32)
+            value = here * infos[s, 0:1, :]
+            for d in range(1, HALO):
+                shifted = pltpu.roll(jnp.where(lane >= d, here, after), shard_len - d, 1)
+                value = value + shifted * infos[s, d : d + 1, :]
+            resampled[s] = value
+            return total + value
+
+        total = lax.fori_loop(0, n, resample, jnp.zeros((stripe, shard_len), jnp.float32))
+        centre = jnp.sum(total, axis=1, keepdims=True) / count
+        for s in range(n):
+            clean[k, :, s * shard_len : (s + 1) * shard_len] = (
+                infos[s, HALO : HALO + 1, :] * (resampled[s] - centre)
+            ).astype(clean.dtype)
+        pltpu.make_async_copy(clean.at[k], cleaned.at[k], clean_sem.at[k]).start()
+        result = jnp.dot(clean[k], table[...], preferred_element_type=jnp.float32)
+        for q in range(bands):
+            spectra[k, q] = result[:, q * 2 * FB : (q + 1) * 2 * FB].astype(spectra.dtype)
+            to = q * BLOCKS + k
+
+            @pl.when(to == me)
+            def _():
+                own[me] = spectra[k, q]
+
+            @pl.when(to != me)
+            def _():
+                pltpu.make_async_remote_copy(
+                    src_ref=spectra.at[k, q],
+                    dst_ref=own.at[me],
+                    send_sem=spec_send,
+                    recv_sem=spec_recv,
+                    device_id={"band": to},
+                    device_id_type=MESH,
+                ).start()
+
+        @pl.when(my_block == k + 1)
+        def _():
+            wait_own()
+            pass_on().start()
+
+        return carry
+
+    def wait_own():
+        pltpu.make_async_copy(own.at[others], own.at[others], spec_recv).wait()
+
+    def pass_on():
+        return pltpu.make_async_remote_copy(
+            src_ref=own,
+            dst_ref=following,
+            send_sem=pass_send,
+            recv_sem=pass_recv,
+            device_id={"band": lax.rem(me + n - 1, n)},
+            device_id_type=MESH,
+        )
+
+    lax.fori_loop(0, BLOCKS, one_block, 0)
+
+    @pl.when(my_block == 0)
+    def _():
+        wait_own()
+
+    @pl.when(my_block != 0)
+    def _():
+        pass_on().wait_send()
+
+    @pl.when(my_block == BLOCKS - 1)
+    def _():
+        following[...] = jnp.zeros_like(following)
+
+    @pl.when(my_block != BLOCKS - 1)
+    def _():
+        pltpu.make_async_copy(following, following, pass_recv).wait()
+
+    own_out[...] = own[...]
+    next_out[...] = following[...]
+
+    def finish(k, carry):
+        pltpu.make_async_copy(clean.at[k], cleaned.at[k], clean_sem.at[k]).wait()
+        return carry
+
+    lax.fori_loop(0, BLOCKS, finish, 0)
+    sent = records.at[pl.ds(0, (n - 1) * BLOCKS * stripe)]
+    pltpu.make_async_copy(sent, sent, raw_send).wait()
+    pltpu.make_async_copy(infos.at[others], infos.at[others], info_send).wait()
+    pltpu.make_async_copy(own.at[others], own.at[others], spec_send).wait()
+
+
+def exchange(records, source, weight, gap_mask, n):
+    channels, shard_len = records.shape
+    stripe = channels // BLOCKS // n
+    bands = n // BLOCKS
+    span = n * shard_len
+    vmem = pl.BlockSpec(memory_space=pltpu.VMEM)
+    hbm = pl.BlockSpec(memory_space=pl.ANY)
+    gathered = jax.ShapeDtypeStruct((n, stripe, 2 * FB), jnp.bfloat16)
+    dma = pltpu.SemaphoreType.DMA
+    return pl.pallas_call(
+        functools.partial(exchange_kernel, n),
+        out_shape=(
+            jax.ShapeDtypeStruct((BLOCKS, stripe, span), jnp.bfloat16),
+            gathered,
+            gathered,
+        ),
+        in_specs=[hbm, vmem, vmem, vmem],
+        out_specs=(hbm, vmem, vmem),
+        scratch_shapes=[
+            pltpu.VMEM((2 * HALO, shard_len), jnp.float32),
+            pltpu.VMEM((n, 2 * HALO, shard_len), jnp.float32),
+            pltpu.VMEM((BLOCKS, n + 1, stripe, shard_len), jnp.bfloat16),
+            pltpu.VMEM((n, stripe, shard_len), jnp.float32),
+            pltpu.VMEM((BLOCKS, stripe, span), jnp.bfloat16),
+            pltpu.VMEM((span, 2 * FB * bands), jnp.bfloat16),
+            pltpu.VMEM((BLOCKS, bands, stripe, 2 * FB), jnp.bfloat16),
+            pltpu.VMEM((n, stripe, 2 * FB), jnp.bfloat16),
+            pltpu.VMEM((n, stripe, 2 * FB), jnp.bfloat16),
+            dma,
+            dma,
+            dma,
+            dma((BLOCKS,)),
+            dma((BLOCKS,)),
+            dma((BLOCKS,)),
+            dma,
+            dma,
+            dma,
+            dma,
+        ],
+        compiler_params=pltpu.CompilerParams(
+            collective_id=0, has_side_effects=True, vmem_limit_bytes=40 * 2**20
+        ),
+        name="exchange",
+    )(records, source.reshape(1, -1), weight.reshape(1, -1), gap_mask.reshape(1, -1))
+
+
+def tiles_kernel(own, following, cleaned, tiles, cleaned_out, left, right, sem):
+    pair, part, rows = pl.program_id(0), pl.program_id(1), pl.program_id(2)
+    first = (pair == 0) & (part == 0) & (rows == 0)
+    last = (pair == 1) & (part == 1) & (rows == pl.num_programs(2) - 1)
+
+    @pl.when(first)
+    def _():
+        pltpu.make_async_copy(cleaned, cleaned_out, sem).start()
+        negate = lax.broadcasted_iota(jnp.int32, own.shape, 1) >= FB
+        for p, block in enumerate((own, following)):
+            values = block[...].astype(jnp.float32)
+            band_power = jnp.sum(values * values, axis=1, keepdims=True) / FB
+            white = (values * lax.rsqrt(band_power + epsilon)).astype(jnp.bfloat16)
+            if p == 0:
+                left[...] = white
+            right[2 * p] = white
+            turned = pltpu.roll(white.astype(jnp.float32), FB, 1)
+            right[2 * p + 1] = jnp.where(negate, -turned, turned).astype(jnp.bfloat16)
+
+    height = tiles.shape[3]
+    start = pl.multiple_of(rows * height, height)
+    product = lax.dot_general(
+        left[pl.ds(start, height), :],
+        right[2 * pair + part],
+        (((1,), (1,)), ((), ())),
+        preferred_element_type=jnp.float32,
+    )
+    tiles[0, 0, 0] = (product * (1.0 / FB)).astype(tiles.dtype)
+
+    @pl.when(last)
+    def _():
+        pltpu.make_async_copy(cleaned, cleaned_out, sem).wait()
+
+
+def make_tiles(own, following, cleaned):
+    width = own.shape[0]
+    height = min(512, width)
+    vmem = pl.BlockSpec(memory_space=pltpu.VMEM)
+    hbm = pl.BlockSpec(memory_space=pl.ANY)
+    return pl.pallas_call(
+        tiles_kernel,
+        grid=(2, 2, width // height),
+        out_shape=(
+            jax.ShapeDtypeStruct((1, 2, 2, width, width), jnp.bfloat16),
+            jax.ShapeDtypeStruct(cleaned.shape, cleaned.dtype),
+        ),
+        in_specs=[vmem, vmem, hbm],
+        out_specs=(
+            pl.BlockSpec((1, 1, 1, height, width), lambda p, c, r: (0, p, c, r, 0)),
+            hbm,
+        ),
+        scratch_shapes=[
+            pltpu.VMEM((width, 2 * FB), jnp.bfloat16),
+            pltpu.VMEM((4, width, 2 * FB), jnp.bfloat16),
+            pltpu.SemaphoreType.DMA,
+        ],
+        compiler_params=pltpu.CompilerParams(vmem_limit_bytes=32 * 2**20),
+        name="tiles",
+    )(own, following, cleaned)
+
+
+def per_device(records, source, weight, gap_mask):
+    n = lax.axis_size("band")
+    channels, shard_len = records.shape
+    stripe = channels // BLOCKS // n
+    span = n * shard_len
+    if stripe % 16 or shard_len != 128 or span & (span - 1) or span > 4096:
+        return per_device_collectives(records, source, weight, gap_mask)
+    cleaned, own, following = exchange(records, source, weight, gap_mask, n)
+    width = n * stripe
+    tiles, cleaned = make_tiles(own.reshape(width, -1), following.reshape(width, -1), cleaned)
+    return cleaned, tiles
+
+
 def solution(mesh):
     placed = (
         P(None, ("groups", "band")),

time: 201 us -> 82.4 us (0.41)
  Pallas kernels: 0 us -> 77.3 us
  blocking collectives: 57.7 us -> 0 us
  waiting for transfers between devices: 53.9 us -> 0 us
  local copies, waits for them, and re-layouts: 31.4 us -> 3.55 us
  starting transfers between devices: 23.9 us -> 0 us
  other arithmetic: 16.5 us -> 0 us
  matrix products: 16.2 us -> 0 us
    pallas_call x0 -> x2, Pallas kernels: none -> 77.3 us  [the longest x1 70.6 us: exchange(): pl.pallas_call(functools.partial(exchange_kernel, n), out_shape=(jax.Shap...]
    psum x1 -> x0, blocking collectives: 57.7 us -> none  [per_device(): lax.psum((jnp.sum(resampled, axis=1), jnp.sum(mask_float)), 'band')]
    all_to_all x2 -> x0, waiting for transfers between devices: 48.7 us -> none  [the longest x1 41.5 us: per_device(): lax.all_to_all(local_clean.reshape(BLOCKS, block_width, shard_len), 'band...]
    all_to_all x2 -> x0, starting transfers between devices: 19.4 us -> none  [the longest x1 10.8 us: per_device(): lax.all_to_all(band_parts.reshape(devices, 2, FB, stripe_width), 'band',...]
    dot_general x4 -> x0, matrix products: 16.2 us -> none  [the longest x1 7.04 us: per_device(): resampled = jnp.dot(padded, spreader, precision=lax.Precision.HIGHEST)]
    unnamed x17 -> x8, local copies, waits for them, and re-layouts: 18 us -> 3.55 us
    another operation x3 -> x0, other arithmetic: 5.28 us -> none
    all_to_all x2 -> x0, local copies, waits for them, and re-layouts: 5.23 us -> none  [per_device(): lax.all_to_all(local_clean.reshape(BLOCKS, block_width, shard_len), 'band...]
  transfers between devices with their start and end apart: 4 -> 0, of which waited for: 4 -> 0; matrix products, arithmetic and copies ran while one was open for 4% -> 0% of each run, Pallas kernels for 0% -> 0%
where the time goes in v1:
time: 82.4 us; the launch traced here: 81.5 us
  Pallas kernels  77.3 us (94%)
  local copies, waits for them, and re-layouts  3.55 us (4%)
    pallas_call x1, Pallas kernels, exchange(): pl.pallas_call(functools.partial(exchange_kernel, n), out_shape=(jax.Shap...  70.6 us
    pallas_call x1, Pallas kernels, make_tiles(): pl.pallas_call(tiles_kernel, grid=(2, 2, width // height), out_shape=(jax...  6.68 us
    unnamed x8, local copies, waits for them, and re-layouts  3.55 us

profile of v1, /device:TPU:1, one launch (start us, length us, event | category | flops | bytes accessed | tf_op | source)
XLA Modules:
  0.0 81.5 jit_solution(10610490043122530157)
XLA Ops:
  0.6 0.0 copy-start
  0.6 1.6 %copy-done = bf16[8192,128]{1,0:T(8,128)(2,1)S(1)} copy-done((bf16[8192,128]{1,0:T(8,128)(2,1)S(1)}, bf16[8192,128]{1,0:T(8,128)(2,1)}, u32[]{:S(2)}) %copy-start) | copy-done | bytes 2097176
  2.2 0.0 copy-start.1
  2.2 0.7 copy-done.1
  2.9 0.0 copy-start.2
  2.9 0.7 copy-done.2
  3.5 0.0 copy-start.3
  3.5 0.7 copy-done.3
  4.2 70.6 %exchange.1 = (bf16[8,64,2048]{2,1,0:T(8,128)(2,1)S(1)}, bf16[16,64,128]{2,1,0:T(8,128)(2,1)S(1)}, bf16[16,64,128]{2,1,0:T(8,128)(2,1)S(1)}) custom-call(bf16[8192,128]{1,0:T(8,128)(2,1)S(1)} %copy-done, s32[1,128]{1,0:T(1,128)S(1)} %bitcast.7, f32[1,128]{1,0:T(1,128)S(1)} %bitcast.8, s32[1,128]{1,0:T(1,128)S(1)} %bitcast.9), custom_call_target="tpu_custom_call" | custom-call | tf_op jit(solution)/shard_map/exchange/pallas_call | solution.py:378
  74.8 6.7 %tiles.1 = (bf16[1,2,2,1024,1024]{4,3,2,1,0:T(8,128)(2,1)}, bf16[8,64,2048]{2,1,0:T(8,128)(2,1)}) custom-call(bf16[1024,128]{1,0:T(8,128)(2,1)S(1)} %bitcast.5, bf16[1024,128]{1,0:T(8,128)(2,1)S(1)} %bitcast.6, bf16[8,64,2048]{2,1,0:T(8,128)(2,1)S(1)} %get-tuple-element.9.cleaned), custom_call_target="tpu_custom_call" | custom-call | tf_op jit(solution)/shard_map/tiles/pallas_call | solution.py:454
Async XLA Ops:
  0.6 1.6 %copy-start = (bf16[8192,128]{1,0:T(8,128)(2,1)S(1)}, bf16[8192,128]{1,0:T(8,128)(2,1)}, u32[]{:S(2)}) copy-start(bf16[8192,128]{1,0:T(8,128)(2,1)} %records.1) | copy-start | bytes 6291460
  2.2 0.7 copy-start.1
  2.9 0.7 copy-start.2
  3.5 0.7 copy-start.3

commit v2 on v1

--- a/solution.py
+++ b/solution.py
@@ -124,6 +124,7 @@
 
 
 LOOKAHEAD = 3
+PASS_DELAY = 2
 MESH = pl.DeviceIdType.MESH
 
 
@@ -139,13 +140,19 @@
 
 def exchange_kernel(
     n,
+    records_in,
+    source_in,
+    weight_in,
+    gap_mask_in,
+    cleaned,
+    own_out,
+    next_out,
     records,
     source,
     weight,
     gap_mask,
-    cleaned,
-    own_out,
-    next_out,
+    small_sem,
+    fetch_sem,
     info,
     infos,
     raw,
@@ -165,6 +172,7 @@
     spec_recv,
     pass_send,
     pass_recv,
+    out_sem,
 ):
     me = lax.axis_index("band")
     shard_len = records.shape[1]
@@ -184,6 +192,24 @@
 
     lax.fori_loop(1, n, greet, 0)
 
+    small = [
+        pltpu.make_async_copy(there, here, small_sem.at[a])
+        for a, (there, here) in enumerate(
+            ((source_in, source), (weight_in, weight), (gap_mask_in, gap_mask))
+        )
+    ]
+    for copy in small:
+        copy.start()
+
+    def fetch(k):
+        rows = pl.ds(pl.multiple_of(k * block_width, block_width), block_width)
+        return pltpu.make_async_copy(records_in.at[rows], records.at[rows], fetch_sem.at[k])
+
+    for k in range(BLOCKS - 1, -1, -1):
+        fetch(k).start()
+    for copy in small:
+        copy.wait()
+
     row = lax.broadcasted_iota(jnp.int32, (HALO, shard_len), 0)
     lane = lax.broadcasted_iota(jnp.int32, (HALO, shard_len), 1)
     offset = source[...] - lane
@@ -201,11 +227,6 @@
             records.at[pl.ds(start, stripe)], raw.at[k, me], raw_local.at[k]
         )
 
-    def start_local(k, carry):
-        local_copy(k).start()
-        return carry
-
-    lax.fori_loop(0, BLOCKS, start_local, 0)
     pl.semaphore_wait(barrier, n - 1)
 
     def send_info(j, carry):
@@ -219,11 +240,17 @@
         ).start()
         return carry
 
-    lax.fori_loop(1, n, send_info, 0)
 
     def send_block(k):
+        fetch(k).wait()
+        local_copy(k).start()
+
         def send(j, carry):
-            to = lax.rem(me + j, n)
+            turn = (j % 2) * (n // 2) + j // 2
+            to, bit = 0, 1
+            while bit < n:
+                to = to + bit * ((me // bit + turn // bit) % 2)
+                bit *= 2
             start = pl.multiple_of(k * block_width + to * stripe, stripe)
             pltpu.make_async_remote_copy(
                 src_ref=records.at[pl.ds(start, stripe)],
@@ -237,7 +264,9 @@
 
         lax.fori_loop(1, n, send, 0)
 
-    for k in range(BLOCKS - 1, BLOCKS - 1 - LOOKAHEAD, -1):
+    send_block(BLOCKS - 1)
+    lax.fori_loop(1, n, send_info, 0)
+    for k in range(BLOCKS - 2, BLOCKS - 1 - LOOKAHEAD, -1):
         send_block(k)
 
     for k in range(BLOCKS):
@@ -277,7 +306,7 @@
         pltpu.make_async_copy(raw.at[k, others], raw.at[k, others], raw_recv.at[k]).wait()
         local_copy(k).wait()
 
-        def resample(s, total):
+        def resample_one(s, total):
             here = raw[k, s].astype(jnp.float32)
             after = raw[k, s + 1].astype(jnp.float32)
             value = here * infos[s, 0:1, :]
@@ -287,7 +316,12 @@
             resampled[s] = value
             return total + value
 
-        total = lax.fori_loop(0, n, resample, jnp.zeros((stripe, shard_len), jnp.float32))
+        def resample(group, total):
+            for s in range(4):
+                total = resample_one(4 * group + s, total)
+            return total
+
+        total = lax.fori_loop(0, n // 4, resample, jnp.zeros((stripe, shard_len), jnp.float32))
         centre = jnp.sum(total, axis=1, keepdims=True) / count
         for s in range(n):
             clean[k, :, s * shard_len : (s + 1) * shard_len] = (
@@ -314,7 +348,7 @@
                     device_id_type=MESH,
                 ).start()
 
-        @pl.when(my_block == k + 1)
+        @pl.when(my_block == k + PASS_DELAY)
         def _():
             wait_own()
             pass_on().start()
@@ -336,9 +370,13 @@
 
     lax.fori_loop(0, BLOCKS, one_block, 0)
 
-    @pl.when(my_block == 0)
+    @pl.when(my_block < PASS_DELAY)
     def _():
         wait_own()
+
+    @pl.when((my_block != 0) & (my_block < PASS_DELAY))
+    def _():
+        pass_on().start()
 
     @pl.when(my_block != 0)
     def _():
@@ -352,8 +390,14 @@
     def _():
         pltpu.make_async_copy(following, following, pass_recv).wait()
 
-    own_out[...] = own[...]
-    next_out[...] = following[...]
+    outs = [
+        pltpu.make_async_copy(own, own_out, out_sem.at[0]),
+        pltpu.make_async_copy(following, next_out, out_sem.at[1]),
+    ]
+    for copy in outs:
+        copy.start()
+    for copy in outs:
+        copy.wait()
 
     def finish(k, carry):
         pltpu.make_async_copy(clean.at[k], cleaned.at[k], clean_sem.at[k]).wait()
@@ -371,7 +415,6 @@
     stripe = channels // BLOCKS // n
     bands = n // BLOCKS
     span = n * shard_len
-    vmem = pl.BlockSpec(memory_space=pltpu.VMEM)
     hbm = pl.BlockSpec(memory_space=pl.ANY)
     gathered = jax.ShapeDtypeStruct((n, stripe, 2 * FB), jnp.bfloat16)
     dma = pltpu.SemaphoreType.DMA
@@ -382,9 +425,15 @@
             gathered,
             gathered,
         ),
-        in_specs=[hbm, vmem, vmem, vmem],
-        out_specs=(hbm, vmem, vmem),
+        in_specs=[hbm, hbm, hbm, hbm],
+        out_specs=(hbm, hbm, hbm),
         scratch_shapes=[
+            pltpu.VMEM(records.shape, records.dtype),
+            pltpu.VMEM((1, shard_len), jnp.int32),
+            pltpu.VMEM((1, shard_len), jnp.float32),
+            pltpu.VMEM((1, shard_len), jnp.int32),
+            dma((3,)),
+            dma((BLOCKS,)),
             pltpu.VMEM((2 * HALO, shard_len), jnp.float32),
             pltpu.VMEM((n, 2 * HALO, shard_len), jnp.float32),
             pltpu.VMEM((BLOCKS, n + 1, stripe, shard_len), jnp.bfloat16),
@@ -404,71 +453,84 @@
             dma,
             dma,
             dma,
+            dma((2,)),
         ],
         compiler_params=pltpu.CompilerParams(
-            collective_id=0, has_side_effects=True, vmem_limit_bytes=40 * 2**20
+            collective_id=0, has_side_effects=True, vmem_limit_bytes=60 * 2**20
         ),
         name="exchange",
     )(records, source.reshape(1, -1), weight.reshape(1, -1), gap_mask.reshape(1, -1))
 
 
-def tiles_kernel(own, following, cleaned, tiles, cleaned_out, left, right, sem):
-    pair, part, rows = pl.program_id(0), pl.program_id(1), pl.program_id(2)
-    first = (pair == 0) & (part == 0) & (rows == 0)
-    last = (pair == 1) & (part == 1) & (rows == pl.num_programs(2) - 1)
-
-    @pl.when(first)
-    def _():
-        pltpu.make_async_copy(cleaned, cleaned_out, sem).start()
-        negate = lax.broadcasted_iota(jnp.int32, own.shape, 1) >= FB
-        for p, block in enumerate((own, following)):
-            values = block[...].astype(jnp.float32)
-            band_power = jnp.sum(values * values, axis=1, keepdims=True) / FB
-            white = (values * lax.rsqrt(band_power + epsilon)).astype(jnp.bfloat16)
-            if p == 0:
-                left[...] = white
-            right[2 * p] = white
-            turned = pltpu.roll(white.astype(jnp.float32), FB, 1)
-            right[2 * p + 1] = jnp.where(negate, -turned, turned).astype(jnp.bfloat16)
-
-    height = tiles.shape[3]
-    start = pl.multiple_of(rows * height, height)
-    product = lax.dot_general(
-        left[pl.ds(start, height), :],
-        right[2 * pair + part],
-        (((1,), (1,)), ((), ())),
-        preferred_element_type=jnp.float32,
-    )
-    tiles[0, 0, 0] = (product * (1.0 / FB)).astype(tiles.dtype)
-
-    @pl.when(last)
-    def _():
-        pltpu.make_async_copy(cleaned, cleaned_out, sem).wait()
+def tiles_kernel(own_in, next_in, cleaned, tiles, cleaned_out, raw, left, right, clean, made, sems):
+    tile_sem, raw_sem, clean_sem = sems
+    fetches = [
+        pltpu.make_async_copy(block, raw.at[p], raw_sem.at[p])
+        for p, block in enumerate((own_in, next_in))
+    ]
+    for copy in fetches:
+        copy.start()
+    clean_fetch = pltpu.make_async_copy(cleaned, clean, clean_sem.at[0])
+    clean_store = pltpu.make_async_copy(clean, cleaned_out, clean_sem.at[1])
+    clean_fetch.start()
+    negate = lax.broadcasted_iota(jnp.int32, raw.shape[1:], 1) >= FB
+
+    def store(p, part):
+        t = 2 * p + part
+        return pltpu.make_async_copy(made.at[t], tiles.at[0, p, part], tile_sem.at[t])
+
+    for p in range(2):
+        fetches[p].wait()
+        values = raw[p].astype(jnp.float32)
+        band_power = jnp.sum(values * values, axis=1, keepdims=True) / FB
+        white = (values * lax.rsqrt(band_power + epsilon)).astype(jnp.bfloat16)
+        if p == 0:
+            left[...] = white
+        right[0] = white
+        turned = pltpu.roll(white.astype(jnp.float32), FB, 1)
+        right[1] = jnp.where(negate, -turned, turned).astype(jnp.bfloat16)
+
+        def make(part, carry):
+            product = lax.dot_general(
+                left[...],
+                right[part],
+                (((1,), (1,)), ((), ())),
+                preferred_element_type=jnp.float32,
+            )
+            made[2 * p + part] = (product * (1.0 / FB)).astype(made.dtype)
+            store(p, part).start()
+            return carry
+
+        lax.fori_loop(0, 2, make, 0)
+        if p == 0:
+            clean_fetch.wait()
+            clean_store.start()
+    for t in range(4):
+        store(t // 2, t % 2).wait()
+    clean_store.wait()
 
 
 def make_tiles(own, following, cleaned):
     width = own.shape[0]
-    height = min(512, width)
-    vmem = pl.BlockSpec(memory_space=pltpu.VMEM)
     hbm = pl.BlockSpec(memory_space=pl.ANY)
+    dma = pltpu.SemaphoreType.DMA
     return pl.pallas_call(
         tiles_kernel,
-        grid=(2, 2, width // height),
         out_shape=(
             jax.ShapeDtypeStruct((1, 2, 2, width, width), jnp.bfloat16),
             jax.ShapeDtypeStruct(cleaned.shape, cleaned.dtype),
         ),
-        in_specs=[vmem, vmem, hbm],
-        out_specs=(
-            pl.BlockSpec((1, 1, 1, height, width), lambda p, c, r: (0, p, c, r, 0)),
-            hbm,
-        ),
+        in_specs=[hbm, hbm, hbm],
+        out_specs=(hbm, hbm),
         scratch_shapes=[
+            pltpu.VMEM((2, width, 2 * FB), jnp.bfloat16),
             pltpu.VMEM((width, 2 * FB), jnp.bfloat16),
-            pltpu.VMEM((4, width, 2 * FB), jnp.bfloat16),
-            pltpu.SemaphoreType.DMA,
+            pltpu.VMEM((2, width, 2 * FB), jnp.bfloat16),
+            pltpu.VMEM(cleaned.shape, cleaned.dtype),
+            pltpu.VMEM((4, width, width), jnp.bfloat16),
+            (dma((4,)), dma((2,)), dma((2,))),
         ],
-        compiler_params=pltpu.CompilerParams(vmem_limit_bytes=32 * 2**20),
+        compiler_params=pltpu.CompilerParams(vmem_limit_bytes=60 * 2**20),
         name="tiles",
     )(own, following, cleaned)
 

time: 82.4 us -> 74.4 us (0.903)
  Pallas kernels: 77.3 us -> 73.6 us
  local copies, waits for them, and re-layouts: 3.55 us -> 0 us
    unnamed x8 -> x0, local copies, waits for them, and re-layouts: 3.55 us -> none
    pallas_call x1, Pallas kernels: 70.6 us -> 67.6 us  [exchange(): pl.pallas_call(functools.partial(exchange_kernel, n), out_shape=(jax.Shap...]
where the time goes in v2:
time: 74.4 us; the launch traced here: 74.3 us
  Pallas kernels  73.6 us (99%)
    pallas_call x1, Pallas kernels, exchange(): pl.pallas_call(functools.partial(exchange_kernel, n), out_shape=(jax.Shap...  67.6 us
    pallas_call x1, Pallas kernels, make_tiles(): pl.pallas_call(tiles_kernel, out_shape=(jax.ShapeDtypeStruct((1, 2, 2, wi...  6.01 us

profile of v2, /device:TPU:1, one launch (start us, length us, event | category | flops | bytes accessed | tf_op | source)
XLA Modules:
  0.0 74.3 jit_solution(12368067473768151917)
XLA Ops:
  0.6 67.6 %exchange.1 = (bf16[8,64,2048]{2,1,0:T(8,128)(2,1)}, bf16[16,64,128]{2,1,0:T(8,128)(2,1)}, bf16[16,64,128]{2,1,0:T(8,128)(2,1)}) custom-call(bf16[8192,128]{1,0:T(8,128)(2,1)} %records_in.1, s32[1,128]{1,0:T(1,128)} %bitcast.7, f32[1,128]{1,0:T(1,128)} %bitcast.8, s32[1,128]{1,0:T(1,128)} %bitcast.9), custom_call_target="tpu_custom_call" | custom-call | tf_op jit(solution)/shard_map/exchange/pallas_call | solution.py:421
  68.3 6.0 %tiles.1 = (bf16[1,2,2,1024,1024]{4,3,2,1,0:T(8,128)(2,1)}, bf16[8,64,2048]{2,1,0:T(8,128)(2,1)}) custom-call(bf16[1024,128]{1,0:T(8,128)(2,1)} %bitcast.5, bf16[1024,128]{1,0:T(8,128)(2,1)} %bitcast.6, bf16[8,64,2048]{2,1,0:T(8,128)(2,1)} %get-tuple-element.9.cleaned), custom_call_target="tpu_custom_call" | custom-call | tf_op jit(solution)/shard_map/tiles/pallas_call | solution.py:517

commit v3 on v2

--- a/solution.py
+++ b/solution.py
@@ -123,7 +123,7 @@
     return (cleaned, pair_tiles(own_block, following)[None])
 
 
-LOOKAHEAD = 3
+LOOKAHEAD = 2
 PASS_DELAY = 2
 MESH = pl.DeviceIdType.MESH
 
@@ -172,6 +172,8 @@
     spec_recv,
     pass_send,
     pass_recv,
+    direct_send,
+    direct_recv,
     out_sem,
 ):
     me = lax.axis_index("band")
@@ -181,6 +183,7 @@
     bands = n // BLOCKS
     span = n * shard_len
     my_block = lax.rem(me, BLOCKS)
+    last = BLOCKS - 1
 
     barrier = pltpu.get_barrier_semaphore()
 
@@ -205,7 +208,7 @@
         rows = pl.ds(pl.multiple_of(k * block_width, block_width), block_width)
         return pltpu.make_async_copy(records_in.at[rows], records.at[rows], fetch_sem.at[k])
 
-    for k in range(BLOCKS - 1, -1, -1):
+    for k in range(BLOCKS):
         fetch(k).start()
     for copy in small:
         copy.wait()
@@ -264,9 +267,9 @@
 
         lax.fori_loop(1, n, send, 0)
 
-    send_block(BLOCKS - 1)
+    send_block(0)
     lax.fori_loop(1, n, send_info, 0)
-    for k in range(BLOCKS - 2, BLOCKS - 1 - LOOKAHEAD, -1):
+    for k in range(1, LOOKAHEAD):
         send_block(k)
 
     for k in range(BLOCKS):
@@ -296,12 +299,10 @@
 
     lane = lax.broadcasted_iota(jnp.int32, (stripe, shard_len), 1)
 
-    def one_block(i, carry):
-        k = BLOCKS - 1 - i
-
-        @pl.when(k >= LOOKAHEAD)
+    def one_block(k, carry):
+        @pl.when(k + LOOKAHEAD < BLOCKS)
         def _():
-            send_block(k - LOOKAHEAD)
+            send_block(k + LOOKAHEAD)
 
         pltpu.make_async_copy(raw.at[k, others], raw.at[k, others], raw_recv.at[k]).wait()
         local_copy(k).wait()
@@ -348,7 +349,7 @@
                     device_id_type=MESH,
                 ).start()
 
-        @pl.when(my_block == k + PASS_DELAY)
+        @pl.when((my_block == k - PASS_DELAY) & (my_block > 0))
         def _():
             wait_own()
             pass_on().start()
@@ -368,27 +369,57 @@
             device_id_type=MESH,
         )
 
+    def direct(q):
+        return pltpu.make_async_remote_copy(
+            src_ref=spectra.at[last, q],
+            dst_ref=following.at[me],
+            send_sem=direct_send.at[q],
+            recv_sem=direct_recv,
+            device_id={"band": q * BLOCKS + last - 1},
+            device_id_type=MESH,
+        )
+
     lax.fori_loop(0, BLOCKS, one_block, 0)
 
-    @pl.when(my_block < PASS_DELAY)
+    for q in range(bands):
+
+        @pl.when(me != q * BLOCKS + last - 1)
+        def _():
+            direct(q).start()
+
+        @pl.when(me == q * BLOCKS + last - 1)
+        def _():
+            following[me] = spectra[last, q]
+
+    @pl.when((my_block == 0) | (my_block > last - PASS_DELAY))
     def _():
         wait_own()
 
-    @pl.when((my_block != 0) & (my_block < PASS_DELAY))
+    @pl.when((my_block > last - PASS_DELAY) & (my_block < last))
     def _():
         pass_on().start()
 
-    @pl.when(my_block != 0)
+    @pl.when((my_block > 0) & (my_block < last))
     def _():
         pass_on().wait_send()
 
-    @pl.when(my_block == BLOCKS - 1)
+    @pl.when(my_block == last)
     def _():
         following[...] = jnp.zeros_like(following)
 
-    @pl.when(my_block != BLOCKS - 1)
+    @pl.when(my_block == last - 1)
+    def _():
+        pltpu.make_async_copy(following.at[others], following.at[others], direct_recv).wait()
+
+    @pl.when(my_block < last - 1)
     def _():
         pltpu.make_async_copy(following, following, pass_recv).wait()
+
+    for q in range(bands):
+
+        @pl.when(me != q * BLOCKS + last - 1)
+        def _():
+            direct(q).wait_send()
 
     outs = [
         pltpu.make_async_copy(own, own_out, out_sem.at[0]),
@@ -453,6 +484,8 @@
             dma,
             dma,
             dma,
+            dma((bands,)),
+            dma,
             dma((2,)),
         ],
         compiler_params=pltpu.CompilerParams(

time: 74.4 us -> 72 us (0.968)
  the two profiles are of different devices: /device:TPU:1 before, /device:TPU:11 now
where the time goes in v3:
time: 72 us; the launch traced here: 71.9 us
  Pallas kernels  71.2 us (99%)
    pallas_call x1, Pallas kernels, exchange(): pl.pallas_call(functools.partial(exchange_kernel, n), out_shape=(jax.Shap...  65.2 us
    pallas_call x1, Pallas kernels, make_tiles(): pl.pallas_call(tiles_kernel, out_shape=(jax.ShapeDtypeStruct((1, 2, 2, wi...  6.02 us

profile of v3, /device:TPU:11, one launch (start us, length us, event | category | flops | bytes accessed | tf_op | source)
XLA Modules:
  0.0 71.9 jit_solution(4525742621899072677)
XLA Ops:
  0.6 65.2 %exchange.1 = (bf16[8,64,2048]{2,1,0:T(8,128)(2,1)}, bf16[16,64,128]{2,1,0:T(8,128)(2,1)}, bf16[16,64,128]{2,1,0:T(8,128)(2,1)}) custom-call(bf16[8192,128]{1,0:T(8,128)(2,1)} %records_in.1, s32[1,128]{1,0:T(1,128)} %bitcast.7, f32[1,128]{1,0:T(1,128)} %bitcast.8, s32[1,128]{1,0:T(1,128)} %bitcast.9), custom_call_target="tpu_custom_call" | custom-call | tf_op jit(solution)/shard_map/exchange/pallas_call | solution.py:452
  65.9 6.0 %tiles.1 = (bf16[1,2,2,1024,1024]{4,3,2,1,0:T(8,128)(2,1)}, bf16[8,64,2048]{2,1,0:T(8,128)(2,1)}) custom-call(bf16[1024,128]{1,0:T(8,128)(2,1)} %bitcast.5, bf16[1024,128]{1,0:T(8,128)(2,1)} %bitcast.6, bf16[8,64,2048]{2,1,0:T(8,128)(2,1)} %get-tuple-element.9.cleaned), custom_call_target="tpu_custom_call" | custom-call | tf_op jit(solution)/shard_map/tiles/pallas_call | solution.py:550
